TPU v7x, 32 devices: a whole 2x2x4 slice. The times are simulated.
32 devices in a mesh: pipe: 2 (over core), dp: 16 (over z, y, x).
Axes of the slice: x: 2, y: 2, z: 4, core: 2. Of those that a mesh axis runs over, the one named last changes fastest.
Arguments:
- tokens: bfloat16 [4, 8192, 384], P(None, 'dp'), may hold values from -6 to 6
- centres: float32 [4, 3, 8192], P(None, None, 'dp'), may hold values from -4 to 4
- visible: int32 [4, 8192], P(None, 'dp'), may hold values 0 or 1
- lengths: int32 [4, 128], P(None, 'dp'), may hold values from 0 to 512, as said below
- cotangent: bfloat16 [4, 8192, 384], P(None, 'dp'), may hold values from -6 to 6
- attend_gain: float32 [2, 384], P('pipe'), may hold values from 0.5 to 1.5
- attend_shift: float32 [2, 384], P('pipe'), may hold values from -1.75 to 1.75
- joint_weight: bfloat16 [2, 384, 1152], P('pipe'), may hold values from -0.3125 to 0.3125
- output_weight: bfloat16 [2, 384, 384], P('pipe'), may hold values from -1.25 to 1.25
- output_bias: float32 [2, 384], P('pipe'), may hold values from -1.75 to 1.75
- feed_gain: float32 [2, 384], P('pipe'), may hold values from 0.5 to 1.5
- feed_shift: float32 [2, 384], P('pipe'), may hold values from -1.75 to 1.75
- expand_weight: bfloat16 [2, 384, 1536], P('pipe'), may hold values from -0.3125 to 0.3125
- expand_bias: float32 [2, 1536], P('pipe'), may hold values from -1.75 to 1.75
- reduce_weight: bfloat16 [2, 1536, 384], P('pipe'), may hold values from -0.15625 to 0.15625
- reduce_bias: float32 [2, 384], P('pipe'), may hold values from -1.75 to 1.75
- place_weight: float32 [2, 3, 128], P('pipe'), may hold values from -3.5 to 3.5
- place_bias: float32 [2, 128], P('pipe'), may hold values from -3 to 3
- embed_weight: bfloat16 [2, 128, 384], P('pipe'), may hold values from -0.5 to 0.5
- mask_token: float32 [384], replicated, may hold values from -6 to 6
Outputs:
- phase_out: bfloat16 [2, 4, 8192, 384], P('pipe', None, 'dp')
- phase_in_grad: float32 [2, 4, 8192, 384], P('pipe', None, 'dp')
- attend_gain_grad: float32 [2, 384], P('pipe')
- attend_shift_grad: float32 [2, 384], P('pipe')
- joint_weight_grad: float32 [2, 384, 1152], P('pipe')
- output_weight_grad: float32 [2, 384, 384], P('pipe')
- output_bias_grad: float32 [2, 384], P('pipe')
- feed_gain_grad: float32 [2, 384], P('pipe')
- feed_shift_grad: float32 [2, 384], P('pipe')
- expand_weight_grad: float32 [2, 384, 1536], P('pipe')
- expand_bias_grad: float32 [2, 1536], P('pipe')
- reduce_weight_grad: float32 [2, 1536, 384], P('pipe')
- reduce_bias_grad: float32 [2, 384], P('pipe')
- place_weight_grad: float32 [2, 3, 128], P('pipe')
- place_bias_grad: float32 [2, 128], P('pipe')
- embed_weight_grad: float32 [2, 128, 384], P('pipe')
- mask_token_grad: float32 [384], replicated
Inputs may be any that keep to these rules, and one draw needn't show every extreme that they name: `lengths`: each aligned group of 8 entries (one index of dp in one micro-batch) sums to 512: either one scan of 512 patches followed by zeros, or 8 objects of 33 to 95 patches; every micro-batch holds at least one scan.
All inputs are finite; a program needn't handle non-finite values. No bound on the sum of `visible` on one device may be relied on, other than what follows from the above.
Results may differ from a plain program's by a relative error of at most 0.014.
Values may be sent and summed in bfloat16 or wider, within the bound.
No kernel may reach another device: no remote copies, remote signals or barrier semaphores. Data moves between devices by JAX's collectives and lax.ppermute only.
A program may use at most 256 MiB of HBM per device.

v0:
```python
import jax
import jax.numpy as jnp
from jax import lax
from jax.sharding import PartitionSpec as P

HEADS = 6


NEG_FILL = -1e30
NORM_EPS = 1e-05


def shifted(block, axis, distance):
    devices = range(lax.axis_size(axis))
    route = [(i - distance, i) for i in devices if i - distance in devices]
    return lax.ppermute(block, axis, route)


def matmul(left_side, right_side):
    return jnp.dot(left_side, right_side, preferred_element_type=jnp.float32)


def left_contract(left_side, right_side):
    return lax.dot_general(
        left_side, right_side, (((0,), (0,)), ((), ())), preferred_element_type=jnp.float32
    )


def right_contract(left_side, right_side):
    return lax.dot_general(
        left_side, right_side, (((1,), (1,)), ((), ())), preferred_element_type=jnp.float32
    )


def smooth(values):
    return jax.nn.gelu(values, approximate=True)


def smooth_grad(values, upstream):
    return jax.vjp(smooth, values)[1](upstream)[0]


def norm_forward(values, gain, shift):
    centred = values - jnp.mean(values, -1, keepdims=True)
    inverse = lax.rsqrt(jnp.mean(centred * centred, -1, keepdims=True) + NORM_EPS)
    scaled = centred * inverse
    return (scaled * gain + shift, scaled, inverse)


def norm_backward(upstream, scaled, inverse, gain):
    weighted = upstream * gain
    grad_in = inverse * (
        weighted
        - jnp.mean(weighted, -1, keepdims=True)
        - scaled * jnp.mean(weighted * scaled, -1, keepdims=True)
    )
    return (grad_in, jnp.sum(upstream * scaled, 0), jnp.sum(upstream, 0))


def allowed_mask(object_lengths, key_flags):
    row_count = key_flags.shape[0]
    places = lax.iota(jnp.int32, row_count)
    object_ends = jnp.cumsum(object_lengths)
    segment = jnp.sum((places[:, None] >= object_ends[None, :]).astype(jnp.int32), axis=1)
    same_object = segment[:, None] == segment[None, :]
    return same_object & ((key_flags[None, :] > 0) | (places[:, None] == places[None, :]))


def split_heads(joint, heads):
    row_count = joint.shape[0]
    model_width = joint.shape[1] // 3
    head_size = model_width // heads
    return [
        joint[:, section * model_width : (section + 1) * model_width].reshape(
            row_count, heads, head_size
        )
        for section in range(3)
    ]


def attend(joint, allowed, heads):
    queries, keys_part, values_part = split_heads(joint, heads)
    head_size = queries.shape[2]
    raw_scores = jnp.einsum("qhd,khd->hqk", queries, keys_part, preferred_element_type=jnp.float32)
    scores = jnp.where(allowed[None], raw_scores * head_size ** (-0.5), NEG_FILL)
    row_max = jnp.max(scores, -1, keepdims=True)
    raised = jnp.exp(scores - row_max)
    soft_weights = raised / jnp.sum(raised, -1, keepdims=True)
    soft_low = soft_weights.astype(jnp.bfloat16)
    mixed = jnp.einsum("hqk,khd->qhd", soft_low, values_part, preferred_element_type=jnp.float32)
    return (mixed.reshape(joint.shape[0], -1), soft_weights, soft_low)


def attend_back(joint, soft_weights, soft_low, grad_mixed, heads):
    queries, keys_part, values_part = split_heads(joint, heads)
    head_size = queries.shape[2]
    grad_heads = grad_mixed.reshape(queries.shape)
    grad_values = jnp.einsum(
        "hqk,qhd->khd", soft_low, grad_heads, preferred_element_type=jnp.float32
    )
    grad_soft = jnp.einsum(
        "qhd,khd->hqk", grad_heads, values_part, preferred_element_type=jnp.float32
    )
    grad_scores = soft_weights * (grad_soft - jnp.sum(grad_soft * soft_weights, -1, keepdims=True))
    grad_raw = (grad_scores * head_size ** (-0.5)).astype(jnp.bfloat16)
    grad_queries = jnp.einsum(
        "hqk,khd->qhd", grad_raw, keys_part, preferred_element_type=jnp.float32
    )
    grad_keys = jnp.einsum("hqk,qhd->khd", grad_raw, queries, preferred_element_type=jnp.float32)
    joined = jnp.concatenate([grad_queries, grad_keys, grad_values], axis=1)
    return joined.reshape(joint.shape[0], -1).astype(jnp.bfloat16)


def block_forward(phase_weights, inputs, allowed, heads):
    first_norm, first_scaled, first_inverse = norm_forward(
        inputs, phase_weights[0], phase_weights[1]
    )
    first_low = first_norm.astype(jnp.bfloat16)
    joint = matmul(first_low, phase_weights[2]).astype(jnp.bfloat16)
    mixed, soft_weights, soft_low = attend(joint, allowed, heads)
    mixed_low = mixed.astype(jnp.bfloat16)
    middle = inputs + (matmul(mixed_low, phase_weights[3]) + phase_weights[4])
    second_norm, second_scaled, second_inverse = norm_forward(
        middle, phase_weights[5], phase_weights[6]
    )
    second_low = second_norm.astype(jnp.bfloat16)
    hidden = matmul(second_low, phase_weights[7]) + phase_weights[8]
    act_low = smooth(hidden).astype(jnp.bfloat16)
    result = middle + (matmul(act_low, phase_weights[9]) + phase_weights[10])
    saved = (
        first_scaled,
        first_inverse,
        first_low,
        joint,
        soft_weights,
        soft_low,
        mixed_low,
        second_scaled,
        second_inverse,
        second_low,
        hidden,
        act_low,
    )
    return (result, saved)


def block_backward(phase_weights, inputs, allowed, heads, upstream):
    unused_out, saved = block_forward(phase_weights, inputs, allowed, heads)
    (
        first_scaled,
        first_inverse,
        first_low,
        joint,
        soft_weights,
        soft_low,
        mixed_low,
        second_scaled,
        second_inverse,
        second_low,
        hidden,
        act_low,
    ) = saved
    reduce_low = upstream.astype(jnp.bfloat16)
    reduce_part = left_contract(act_low, reduce_low)
    grad_hidden = smooth_grad(hidden, right_contract(reduce_low, phase_weights[9])).astype(
        jnp.bfloat16
    )
    expand_part = left_contract(second_low, grad_hidden)
    grad_norm, feed_gain_part, feed_shift_part = norm_backward(
        right_contract(grad_hidden, phase_weights[7]),
        second_scaled,
        second_inverse,
        phase_weights[5],
    )
    grad_middle = upstream + grad_norm
    middle_low = grad_middle.astype(jnp.bfloat16)
    output_part = left_contract(mixed_low, middle_low)
    grad_mixed = right_contract(middle_low, phase_weights[3]).astype(jnp.bfloat16)
    grad_joint = attend_back(joint, soft_weights, soft_low, grad_mixed, heads)
    joint_part = left_contract(first_low, grad_joint)
    grad_first, attend_gain_part, attend_shift_part = norm_backward(
        right_contract(grad_joint, phase_weights[2]), first_scaled, first_inverse, phase_weights[0]
    )
    parts = [
        attend_gain_part,
        attend_shift_part,
        joint_part,
        output_part,
        jnp.sum(middle_low.astype(jnp.float32), 0),
        feed_gain_part,
        feed_shift_part,
        expand_part,
        jnp.sum(grad_hidden.astype(jnp.float32), 0),
        reduce_part,
        jnp.sum(reduce_low.astype(jnp.float32), 0),
    ]
    return (grad_middle + grad_first, parts)


def place_forward(phase_weights, centre_block):
    coords = phase_weights[11]
    pre = (
        centre_block[0][:, None] * coords[0][None, :]
        + centre_block[1][:, None] * coords[1][None, :]
        + centre_block[2][:, None] * coords[2][None, :]
        + phase_weights[12]
    )
    act_low = smooth(pre).astype(jnp.bfloat16)
    return (matmul(act_low, phase_weights[13]), pre, act_low)


def place_backward(phase_weights, centre_block, pre, act_low, upstream):
    grad_low = upstream.astype(jnp.bfloat16)
    embed_part = left_contract(act_low, grad_low)
    grad_pre = smooth_grad(pre, right_contract(grad_low, phase_weights[13]))
    place_part = jnp.stack(
        [jnp.sum(centre_block[axis_pick][:, None] * grad_pre, 0) for axis_pick in range(3)]
    )
    return [place_part, jnp.sum(grad_pre, 0), embed_part]


def shards(
    tokens,
    centres,
    visible,
    lengths,
    cotangent,
    attend_gain,
    attend_shift,
    joint_weight,
    output_weight,
    output_bias,
    feed_gain,
    feed_shift,
    expand_weight,
    expand_bias,
    reduce_weight,
    reduce_bias,
    place_weight,
    place_bias,
    embed_weight,
    mask_token,
):
    phase_weights = [
        piece[0]
        for piece in (
            attend_gain,
            attend_shift,
            joint_weight,
            output_weight,
            output_bias,
            feed_gain,
            feed_shift,
            expand_weight,
            expand_bias,
            reduce_weight,
            reduce_bias,
            place_weight,
            place_bias,
            embed_weight,
        )
    ]
    phase = lax.axis_index("pipe")
    encoding = phase == 0
    micro = tokens.shape[0]
    heads = HEADS

    def build(index, received):
        token_block = lax.dynamic_index_in_dim(tokens, index, 0, keepdims=False)
        centre_block = lax.dynamic_index_in_dim(centres, index, 0, keepdims=False)
        visible_block = lax.dynamic_index_in_dim(visible, index, 0, keepdims=False)
        length_block = lax.dynamic_index_in_dim(lengths, index, 0, keepdims=False)
        embedded, pre, act_low = place_forward(phase_weights, centre_block)
        decoded = jnp.where(
            visible_block[:, None] > 0, received.astype(jnp.float32), mask_token[None, :]
        )
        inputs = jnp.where(encoding, token_block.astype(jnp.float32), decoded) + embedded
        key_flags = jnp.where(encoding, visible_block, jnp.ones_like(visible_block))
        return (
            inputs,
            allowed_mask(length_block, key_flags),
            (centre_block, pre, act_low, visible_block),
        )

    received_act = jnp.zeros(tokens.shape[1:], jnp.bfloat16)
    received_grad = jnp.zeros(tokens.shape[1:], jnp.bfloat16)
    out_store = jnp.zeros(tokens.shape, jnp.bfloat16)
    grad_store = jnp.zeros(tokens.shape, jnp.float32)
    totals = [jnp.zeros(piece.shape, jnp.float32) for piece in phase_weights]
    mask_total = jnp.zeros(mask_token.shape, jnp.float32)
    for moment in range(micro + 2):
        fwd_index = moment - phase
        fwd_ok = (fwd_index >= 0) & (fwd_index < micro)
        fwd_safe = jnp.clip(fwd_index, 0, micro - 1)
        arrived_act = received_act

        def run_forward():
            inputs, allowed, unused_cache = build(fwd_safe, arrived_act)
            return block_forward(phase_weights, inputs, allowed, heads)[0].astype(jnp.bfloat16)

        def skip_forward():
            return jnp.zeros(tokens.shape[1:], jnp.bfloat16)

        result = lax.cond(fwd_ok, run_forward, skip_forward)
        kept_out = lax.dynamic_index_in_dim(out_store, fwd_safe, 0, keepdims=False)
        out_store = lax.dynamic_update_index_in_dim(
            out_store, jnp.where(fwd_ok, result, kept_out), fwd_safe, 0
        )
        back_index = moment - 2 + phase
        back_ok = (back_index >= 0) & (back_index < micro)
        back_safe = jnp.clip(back_index, 0, micro - 1)
        arrived_grad = received_grad

        def run_backward():
            back_inputs, back_allowed, place_cache = build(back_safe, arrived_act)
            given = lax.dynamic_index_in_dim(cotangent, back_safe, 0, keepdims=False).astype(
                jnp.float32
            )
            upstream = jnp.where(encoding, arrived_grad.astype(jnp.float32), given)
            grad_inputs, block_parts = block_backward(
                phase_weights, back_inputs, back_allowed, heads, upstream
            )
            place_parts = place_backward(
                phase_weights, place_cache[0], place_cache[1], place_cache[2], grad_inputs
            )
            return (grad_inputs, tuple(block_parts + place_parts))

        def skip_backward():
            return (
                jnp.zeros(tokens.shape[1:], jnp.float32),
                tuple((jnp.zeros(piece.shape, jnp.float32) for piece in phase_weights)),
            )

        grad_inputs, step_parts = lax.cond(back_ok, run_backward, skip_backward)
        totals = [running + addend for running, addend in zip(totals, step_parts)]
        kept_grad = lax.dynamic_index_in_dim(grad_store, back_safe, 0, keepdims=False)
        grad_store = lax.dynamic_update_index_in_dim(
            grad_store, jnp.where(back_ok, grad_inputs, kept_grad), back_safe, 0
        )
        visible_block = lax.dynamic_index_in_dim(visible, back_safe, 0, keepdims=False)
        send_grad = jnp.where(visible_block[:, None] > 0, grad_inputs, 0.0).astype(jnp.bfloat16)
        masked_sum = jnp.sum(jnp.where(visible_block[:, None] > 0, 0.0, grad_inputs), 0)
        mask_total = mask_total + jnp.where(encoding, 0.0, masked_sum)
        received_act = shifted(result, "pipe", 1)
        received_grad = shifted(send_grad, "pipe", -1)
    summed = list(lax.psum(tuple(totals), "dp"))
    mask_grad = lax.psum(mask_total, ("pipe", "dp"))
    return tuple(
        [out_store[None], grad_store[None]] + [piece[None] for piece in summed] + [mask_grad]
    )


def solution(mesh):
    in_specs = (
        P(None, "dp", None),
        P(None, None, "dp"),
        P(None, "dp"),
        P(None, "dp"),
        P(None, "dp", None),
        P("pipe", None),
        P("pipe", None),
        P("pipe", None, None),
        P("pipe", None, None),
        P("pipe", None),
        P("pipe", None),
        P("pipe", None),
        P("pipe", None, None),
        P("pipe", None),
        P("pipe", None, None),
        P("pipe", None),
        P("pipe", None, None),
        P("pipe", None),
        P("pipe", None, None),
        P(),
    )
    out_specs = (
        P("pipe", None, "dp", None),
        P("pipe", None, "dp", None),
        P("pipe", None),
        P("pipe", None),
        P("pipe", None, None),
        P("pipe", None, None),
        P("pipe", None),
        P("pipe", None),
        P("pipe", None),
        P("pipe", None, None),
        P("pipe", None),
        P("pipe", None, None),
        P("pipe", None),
        P("pipe", None, None),
        P("pipe", None),
        P("pipe", None, None),
        P(),
    )
    return jax.shard_map(shards, mesh=mesh, in_specs=in_specs, out_specs=out_specs, check_vma=False)
```

profile of v0, /device:TPU:0, one launch (start us, length us, event | category | flops | bytes accessed | tf_op | source)
XLA Modules:
  0.0 1015.8 jit_solution(6621795357767055495)
XLA Ops:
  7.9 7.6 conditional.18
  20.6 28.9 %conditional.12 = (bf16[512,384]{0,1:T(8,128)(2,1)S(1)}) conditional(s32[]{:T(128)} %convert_element_type.771, () %tuple.92, (pred[]{:T(512)}, s32[]{:T(128)}, bf16[4,512,384]{2,1,0:T(8,128)(2,1)}, s32[4,512]{1,0:T(4,128)S(1)}, f32[384]{0:T(512)}, /*index=5*/f32[4,3,512]{2,0,1:T(4,128)}, f32[3,128]{1,0:T(4,128)S(1)}, f32[1,128]{1,0:T(1,128)}, ...), branch_computations={%region_0.1_spmd, %region_1.10_spmd} | conditional | flops 2290366976 | bytes 35872820 | solution.py:304
  52.9 19.1 %conditional.19 = (f32[384]{0:T(512)}, f32[384]{0:T(512)}, f32[384,1152]{1,0:T(8,128)}, f32[384,384]{1,0:T(8,128)}, f32[384]{0:T(512)}, /*index=5*/f32[384]{0:T(...) conditional(s32[]{:T(128)} %convert_element_type.778, ...), branch_computations={%region_86.87_spmd, %region_87.112_spmd} | conditional | flops 6275154944 | bytes 204758176 | solution.py:334
  75.3 29.3 %conditional.13 = (bf16[512,384]{0,1:T(8,128)(2,1)S(1)}) conditional(s32[]{:T(128)} %convert_element_type.772, () %tuple.94, (pred[]{:T(512)}, s32[]{:T(128)}, bf16[4,512,384]{2,1,0:T(8,128)(2,1)}, s32[4,512]{1,0:T(4,128)}, bf16[512,384]{0,1:T(8,128)(2,1)}, /*index=5*/f32[384]{0:T(512)}, f32[4,3,512]{2,0,1:T(4,128)}, f32[3,128]{1,0:T(4,128)}, ...), branch_computations={%region_10.11_spmd, %region_11.20_spmd} | conditional | flops 2290563584 | bytes 39811180 | solution.py:304
  88.3 6.2 fusion.950
  104.7 91.8 %collective-permute-start.1 = (bf16[512,384]{0,1:T(8,128)(2,1)S(1)}, bf16[512,384]{0,1:T(8,128)(2,1)S(1)}, u32[]{:S(2)}, u32[]{:S(2)}) collective-permute-start(bf16[512,384]{0,1:T(8,128)(2,1)S(1)} %get-tuple-element.2390), channel_id=1, source_target_pairs={{0,16},{1,17},{2,18},{3,19},{4,20},{5,21},{6,22},{7,23},{8,24},{9,... | collective-permute-start | bytes 1179656 | tf_op jit(solution)/shard_map/ppermute | solution.py:16
  198.3 108.8 %conditional.20 = (f32[384]{0:T(512)}, f32[384]{0:T(512)}, f32[384,1152]{1,0:T(8,128)}, f32[384,384]{1,0:T(8,128)}, f32[384]{0:T(512)}, /*index=5*/f32[384]{0:T(...) conditional(s32[]{:T(128)} %convert_element_type.780, ...), branch_computations={%region_112.113_spmd, %region_113.138_spmd} | conditional | flops 6275154944 | bytes 204758176 | solution.py:334
  209.6 6.7 fusion.982
  253.4 11.6 %fusion.616 = bf16[512,6,64]{0,2,1:T(8,128)(2,1)} fusion(bf16[512,6,64]{0,2,1:T(8,128)(2,1)S(1)} %bitcast.757, f32[6,512,512]{1,2,0:T(8,128)} %fusion.1006, f32[6,512,512]{1,2,0:T(8,128)} %get-tuple-element.2099, f32[6,512]{1,0:T(8,128)} %get-tuple-element.2098), kind=kOutput, calls=%fused_computation.857 | convolution fusion | flops 212536832 | bytes 13381632 | tf_op jit(solution)/shard_map/cond/branch_1_fun/hqk,khd->qhd/dot_general | solution.py:106
  265.0 11.3 %fusion.613 = bf16[512,6,64]{0,2,1:T(8,128)(2,1)} fusion(bf16[512,6,64]{0,2,1:T(8,128)(2,1)} %bitcast.747, f32[6,512,512]{1,2,0:T(8,128)} %fusion.1006, f32[6,512,512]{1,2,0:T(8,128)} %get-tuple-element.2099, f32[6,512]{1,0:T(8,128)} %get-tuple-element.2098), kind=kOutput, calls=%fused_computation.856 | convolution fusion | flops 212536832 | bytes 13381632 | tf_op jit(solution)/shard_map/cond/branch_1_fun/hqk,qhd->khd/dot_general | solution.py:109
  310.5 29.3 %conditional.14 = (bf16[512,384]{0,1:T(8,128)(2,1)S(1)}) conditional(s32[]{:T(128)} %convert_element_type.773, () %tuple.96, (pred[]{:T(512)}, s32[]{:T(128)}, bf16[4,512,384]{2,1,0:T(8,128)(2,1)}, s32[4,512]{1,0:T(4,128)}, bf16[512,384]{0,1:T(8,128)(2,1)}, /*index=5*/f32[384]{0:T(512)}, f32[4,3,512]{2,0,1:T(4,128)}, f32[3,128]{1,0:T(4,128)}, ...), branch_computations={%region_20.21_spmd, %region_21.30_spmd} | conditional | flops 2290563584 | bytes 39811180 | solution.py:304
  323.4 6.2 fusion.954
  345.6 109.2 %conditional.21 = (f32[384]{0:T(512)}, f32[384]{0:T(512)}, f32[384,1152]{1,0:T(8,128)}, f32[384,384]{1,0:T(8,128)}, f32[384]{0:T(512)}, /*index=5*/f32[384]{0:T(...) conditional(s32[]{:T(128)} %convert_element_type.782, ...), branch_computations={%region_138.139_spmd, %region_139.164_spmd} | conditional | flops 6275154944 | bytes 204758176 | solution.py:334
  357.1 6.7 fusion.988
  401.0 11.6 %fusion.706 = bf16[512,6,64]{0,2,1:T(8,128)(2,1)} fusion(bf16[512,6,64]{0,2,1:T(8,128)(2,1)S(1)} %bitcast.759, f32[6,512,512]{1,2,0:T(8,128)} %fusion.1007, f32[6,512,512]{1,2,0:T(8,128)} %get-tuple-element.2122, f32[6,512]{1,0:T(8,128)} %get-tuple-element.2121), kind=kOutput, calls=%fused_computation.987 | convolution fusion | flops 212536832 | bytes 13381632 | tf_op jit(solution)/shard_map/cond/branch_1_fun/hqk,khd->qhd/dot_general | solution.py:106
  412.6 11.4 %fusion.703 = bf16[512,6,64]{0,2,1:T(8,128)(2,1)} fusion(bf16[512,6,64]{0,2,1:T(8,128)(2,1)} %bitcast.749, f32[6,512,512]{1,2,0:T(8,128)} %fusion.1007, f32[6,512,512]{1,2,0:T(8,128)} %get-tuple-element.2122, f32[6,512]{1,0:T(8,128)} %get-tuple-element.2121), kind=kOutput, calls=%fused_computation.986 | convolution fusion | flops 212536832 | bytes 13381632 | tf_op jit(solution)/shard_map/cond/branch_1_fun/hqk,qhd->khd/dot_general | solution.py:109
  458.2 29.3 %conditional.15 = (bf16[512,384]{0,1:T(8,128)(2,1)S(1)}) conditional(s32[]{:T(128)} %convert_element_type.774, () %tuple.98, (pred[]{:T(512)}, s32[]{:T(128)}, bf16[4,512,384]{2,1,0:T(8,128)(2,1)}, s32[4,512]{1,0:T(4,128)}, bf16[512,384]{0,1:T(8,128)(2,1)}, /*index=5*/f32[384]{0:T(512)}, f32[4,3,512]{2,0,1:T(4,128)}, f32[3,128]{1,0:T(4,128)}, ...), branch_computations={%region_30.31_spmd, %region_31.40_spmd} | conditional | flops 2290563584 | bytes 39811180 | solution.py:304
  471.1 6.2 fusion.958
  493.3 109.2 %conditional.22 = (f32[384]{0:T(512)}, f32[384]{0:T(512)}, f32[384,1152]{1,0:T(8,128)}, f32[384,384]{1,0:T(8,128)}, f32[384]{0:T(512)}, /*index=5*/f32[384]{0:T(...) conditional(s32[]{:T(128)} %convert_element_type.784, ...), branch_computations={%region_164.165_spmd, %region_165.190_spmd} | conditional | flops 6275154944 | bytes 204758176 | solution.py:334
  504.8 6.7 fusion.994
  548.6 11.6 %fusion.796 = bf16[512,6,64]{0,2,1:T(8,128)(2,1)} fusion(bf16[512,6,64]{0,2,1:T(8,128)(2,1)S(1)} %bitcast.761, f32[6,512,512]{1,2,0:T(8,128)} %fusion.1008, f32[6,512,512]{1,2,0:T(8,128)} %get-tuple-element.2145, f32[6,512]{1,0:T(8,128)} %get-tuple-element.2144), kind=kOutput, calls=%fused_computation.1117 | convolution fusion | flops 212536832 | bytes 13381632 | tf_op jit(solution)/shard_map/cond/branch_1_fun/hqk,khd->qhd/dot_general | solution.py:106
  560.2 11.4 %fusion.793 = bf16[512,6,64]{0,2,1:T(8,128)(2,1)} fusion(bf16[512,6,64]{0,2,1:T(8,128)(2,1)} %bitcast.751, f32[6,512,512]{1,2,0:T(8,128)} %fusion.1008, f32[6,512,512]{1,2,0:T(8,128)} %get-tuple-element.2145, f32[6,512]{1,0:T(8,128)} %get-tuple-element.2144), kind=kOutput, calls=%fused_computation.1116 | convolution fusion | flops 212536832 | bytes 13381632 | tf_op jit(solution)/shard_map/cond/branch_1_fun/hqk,qhd->khd/dot_general | solution.py:109
  605.9 33.0 %collective-permute-start.4 = (bf16[512,384]{0,1:T(8,128)(2,1)S(1)}, bf16[512,384]{0,1:T(8,128)(2,1)S(1)}, u32[]{:S(2)}, u32[]{:S(2)}) collective-permute-start(bf16[512,384]{0,1:T(8,128)(2,1)S(1)} %get-tuple-element.2393), channel_id=1, source_target_pairs={{0,16},{1,17},{2,18},{3,19},{4,20},{5,21},{6,22},{7,23},{8,24},{9,... | collective-permute-start | bytes 1179656 | tf_op jit(solution)/shard_map/ppermute | solution.py:16
  641.0 95.5 %conditional.23 = (f32[384]{0:T(512)}, f32[384]{0:T(512)}, f32[384,1152]{1,0:T(8,128)}, f32[384,384]{1,0:T(8,128)}, f32[384]{0:T(512)}, /*index=5*/f32[384]{0:T(...) conditional(s32[]{:T(128)} %convert_element_type.786, ...), branch_computations={%region_190.191_spmd, %region_191.216_spmd} | conditional | flops 6275154944 | bytes 193756192 | solution.py:334
  652.5 6.7 fusion.1000
  688.9 10.9 %fusion.886 = bf16[512,6,64]{0,2,1:T(8,128)(2,1)S(1)} fusion(bf16[512,6,64]{0,2,1:T(8,128)(2,1)S(1)} %bitcast.763, f32[6,512,512]{1,2,0:T(8,128)} %fusion.1009, f32[6,512,512]{1,2,0:T(8,128)} %get-tuple-element.2168, f32[6,512]{1,0:T(8,128)} %get-tuple-element.2167), kind=kOutput, calls=%fused_computation.1247 | convolution fusion | flops 212536832 | bytes 13381632 | tf_op jit(solution)/shard_map/cond/branch_1_fun/hqk,khd->qhd/dot_general | solution.py:106
  699.7 10.5 %fusion.883 = bf16[512,6,64]{0,2,1:T(8,128)(2,1)S(1)} fusion(bf16[512,6,64]{0,2,1:T(8,128)(2,1)} %bitcast.753, f32[6,512,512]{1,2,0:T(8,128)} %fusion.1009, f32[6,512,512]{1,2,0:T(8,128)} %get-tuple-element.2168, f32[6,512]{1,0:T(8,128)} %get-tuple-element.2167), kind=kOutput, calls=%fused_computation.1246 | convolution fusion | flops 212536832 | bytes 13381632 | tf_op jit(solution)/shard_map/cond/branch_1_fun/hqk,qhd->khd/dot_general | solution.py:109
  738.6 7.1 add_bitcast_fusion
  745.7 8.1 add_bitcast_fusion.1
  813.1 42.6 %psum.119 = f32[384]{0:T(512)} all-reduce(f32[384]{0:T(512)S(1)} %select_add_fusion), channel_id=1, replica_groups=mesh['pipe'=2,'dp'=16] {'pipe','dp'}, use_global_device_ids=true, to_apply=%region_236.237 | all-reduce | flops 384 | bytes 3072 | tf_op jit(solution)/shard_map/psum | solution.py:347
  856.5 76.4 %all-reduce = (f32[1,384]{1,0:T(1,128)}, f32[1,384]{1,0:T(1,128)}, f32[1,384]{1,0:T(1,128)}, f32[1,384]{1,0:T(1,128)}, f32[1,384]{1,0:T(1,128)}, /*index=5*/f32[...) all-reduce(f32[1,384]{1,0:T(1,128)} %broadcast_in_dim.645, ...), channel_id=1, replica_groups=mesh['pipe'=2,'dp'=16] {'dp'}, use_global_device_ids=true, to_apply=%region_216.217 | all-reduce | flops 4352 | bytes 34816 | tf_op jit(solution)/shard_map/psum | solution.py:346
  937.0 64.2 %all-reduce.4.cloned.1.call-done = (f32[1,384,1152]{2,1,0:T(8,128)}, f32[1,384,384]{2,1,0:T(8,128)}, f32[1,384,1536]{2,1,0:T(8,128)}, f32[1,1536,384]{2,1,0:T(8,128)}, f32[1,128,384]{2,1,0:T(8,128)}) async-done(((f32[1,384,1152]{2,1,0:T(8,128)}, f32[1,384,384]{2,1,0:T(8,128)}, f32[1,384,1536]{2,1,0:T(8,128)}, f32[1,1536,384]{2,1,0:T(8,128)}, f32[1,128,384]{2,1,0:T(8,128)}), (f32[1,384,1152]{2,1,0:T(8,128)}, ...) | async-done | bytes 7274512 | tf_op jit(solution)/shard_map/psum | solution.py:346
  (1146 shorter events, 532.3 us)
Async XLA Ops:
  7.2 994.0 %all-reduce.4.cloned.1.call-start = ((), (), s32[]{:S(2)}) async-start(), calls=%async_computation | async-start | bytes 14548992 | tf_op jit(solution)/shard_map/psum | solution.py:346
  7.9 44.2 %copy-start.199 = (f32[1,3,128]{2,1,0:T(4,128)}, f32[1,3,128]{2,1,0:T(4,128)S(1)}, u32[]{:S(2)}) copy-start(f32[1,3,128]{2,1,0:T(4,128)S(1)} %copy.569) | copy-start | bytes 4612
  7.9 12.5 %copy-start.202 = (s32[4,512]{1,0:T(4,128)S(1)}, s32[4,512]{1,0:T(4,128)}, u32[]{:S(2)}) copy-start(s32[4,512]{1,0:T(4,128)} %param.46) | copy-start | bytes 24580
  7.9 12.6 %copy-start.213 = (f32[1,384]{1,0:T(1,128)S(1)}, f32[1,384]{1,0:T(1,128)}, u32[]{:S(2)}) copy-start(f32[1,384]{1,0:T(1,128)} %param.59) | copy-start | bytes 4612
  19.2 31.6 %collective-permute-start.5 = (bf16[512,384]{1,0:T(8,128)(2,1)}, bf16[512,384]{1,0:T(8,128)(2,1)}, u32[]{:S(2)}, u32[]{:S(2)}) collective-permute-start(bf16[512,384]{1,0:T(8,128)(2,1)} %select_convert_fusion.4), channel_id=1, source_target_pairs={{16,0},{17,1},{18,2},{19,3},{20,4},{21,5},{22,6},{23,7},{24,8},{25... | collective-permute-start | bytes 1179656 | tf_op jit(solution)/shard_map/ppermute | solution.py:16
  20.5 31.6 %copy-start.13 = (bf16[4,512,384]{2,1,0:T(8,128)(2,1)S(1)}, bf16[4,512,384]{2,1,0:T(8,128)(2,1)}, u32[]{:S(2)}) copy-start(bf16[4,512,384]{2,1,0:T(8,128)(2,1)} %param.48) | copy-start | bytes 4718596
  49.5 2.6 collective-permute-start
  74.0 122.4 %collective-permute-start.6 = (bf16[512,384]{1,0:T(8,128)(2,1)}, bf16[512,384]{1,0:T(8,128)(2,1)}, u32[]{:S(2)}, u32[]{:S(2)}) collective-permute-start(bf16[512,384]{1,0:T(8,128)(2,1)} %select_convert_fusion.3), channel_id=1, source_target_pairs={{16,0},{17,1},{18,2},{19,3},{20,4},{21,5},{22,6},{23,7},{24,8},{25... | collective-permute-start | bytes 1179656 | tf_op jit(solution)/shard_map/ppermute | solution.py:16
  104.6 92.9 %copy-start.66 = (bf16[512,384]{0,1:T(8,128)(2,1)}, bf16[512,384]{0,1:T(8,128)(2,1)S(1)}, u32[]{:S(2)}) copy-start(bf16[512,384]{0,1:T(8,128)(2,1)S(1)} %get-tuple-element.2390) | copy-start | bytes 1179652
  104.7 92.9 %collective-permute-start.1 = (bf16[512,384]{0,1:T(8,128)(2,1)S(1)}, bf16[512,384]{0,1:T(8,128)(2,1)S(1)}, u32[]{:S(2)}, u32[]{:S(2)}) collective-permute-start(bf16[512,384]{0,1:T(8,128)(2,1)S(1)} %get-tuple-element.2390), channel_id=1, source_target_pairs={{0,16},{1,17},{2,18},{3,19},{4,20},{5,21},{6,22},{7,23},{8,24},{9,... | collective-permute-start | bytes 1179656 | tf_op jit(solution)/shard_map/ppermute | solution.py:16
  222.4 23.3 %copy-start.205 = (f32[512]{0:T(512)}, f32[512]{0:T(512)S(1)}, u32[]{:S(2)}) copy-start(f32[512]{0:T(512)S(1)} %broadcast_multiply_fusion.28) | copy-start | bytes 6148 | tf_op jit(solution)/shard_map/cond
  222.6 23.1 %copy-start.231 = (f32[512]{0:T(512)}, f32[512]{0:T(512)S(1)}, u32[]{:S(2)}) copy-start(f32[512]{0:T(512)S(1)} %add_rsqrt_fusion.16) | copy-start | bytes 6148 | tf_op jit(solution)/shard_map/cond
  265.0 11.3 %copy-start.59 = (bf16[512,384]{0,1:T(8,128)(2,1)S(1)}, bf16[512,384]{0,1:T(8,128)(2,1)}, u32[]{:S(2)}) copy-start(bf16[512,384]{0,1:T(8,128)(2,1)} %copy-done.58) | copy-start | bytes 1179652 | tf_op jit(solution)/shard_map/cond
  309.2 34.4 %collective-permute-start.7 = (bf16[512,384]{1,0:T(8,128)(2,1)}, bf16[512,384]{1,0:T(8,128)(2,1)}, u32[]{:S(2)}, u32[]{:S(2)}) collective-permute-start(bf16[512,384]{1,0:T(8,128)(2,1)} %select_convert_fusion.2), channel_id=1, source_target_pairs={{16,0},{17,1},{18,2},{19,3},{20,4},{21,5},{22,6},{23,7},{24,8},{25... | collective-permute-start | bytes 1179656 | tf_op jit(solution)/shard_map/ppermute | solution.py:16
  339.8 5.1 collective-permute-start.2
  369.9 23.4 %copy-start.207 = (f32[512]{0:T(512)}, f32[512]{0:T(512)S(1)}, u32[]{:S(2)}) copy-start(f32[512]{0:T(512)S(1)} %broadcast_multiply_fusion.34) | copy-start | bytes 6148 | tf_op jit(solution)/shard_map/cond
  370.0 23.2 %copy-start.233 = (f32[512]{0:T(512)}, f32[512]{0:T(512)S(1)}, u32[]{:S(2)}) copy-start(f32[512]{0:T(512)S(1)} %add_rsqrt_fusion.18) | copy-start | bytes 6148 | tf_op jit(solution)/shard_map/cond
  412.6 11.4 %copy-start.61 = (bf16[512,384]{0,1:T(8,128)(2,1)S(1)}, bf16[512,384]{0,1:T(8,128)(2,1)}, u32[]{:S(2)}) copy-start(bf16[512,384]{0,1:T(8,128)(2,1)} %copy-done.60) | copy-start | bytes 1179652 | tf_op jit(solution)/shard_map/cond
  456.9 34.4 %collective-permute-start.8 = (bf16[512,384]{1,0:T(8,128)(2,1)}, bf16[512,384]{1,0:T(8,128)(2,1)}, u32[]{:S(2)}, u32[]{:S(2)}) collective-permute-start(bf16[512,384]{1,0:T(8,128)(2,1)} %select_convert_fusion.1), channel_id=1, source_target_pairs={{16,0},{17,1},{18,2},{19,3},{20,4},{21,5},{22,6},{23,7},{24,8},{25... | collective-permute-start | bytes 1179656 | tf_op jit(solution)/shard_map/ppermute | solution.py:16
  487.5 5.1 collective-permute-start.3
  517.5 23.4 %copy-start.209 = (f32[512]{0:T(512)}, f32[512]{0:T(512)S(1)}, u32[]{:S(2)}) copy-start(f32[512]{0:T(512)S(1)} %broadcast_multiply_fusion.40) | copy-start | bytes 6148 | tf_op jit(solution)/shard_map/cond
  517.7 23.3 %copy-start.235 = (f32[512]{0:T(512)}, f32[512]{0:T(512)S(1)}, u32[]{:S(2)}) copy-start(f32[512]{0:T(512)S(1)} %add_rsqrt_fusion.20) | copy-start | bytes 6148 | tf_op jit(solution)/shard_map/cond
  560.2 11.4 %copy-start.63 = (bf16[512,384]{0,1:T(8,128)(2,1)S(1)}, bf16[512,384]{0,1:T(8,128)(2,1)}, u32[]{:S(2)}) copy-start(bf16[512,384]{0,1:T(8,128)(2,1)} %copy-done.62) | copy-start | bytes 1179652 | tf_op jit(solution)/shard_map/cond
  604.5 34.4 %collective-permute-start.9 = (bf16[512,384]{1,0:T(8,128)(2,1)}, bf16[512,384]{1,0:T(8,128)(2,1)}, u32[]{:S(2)}, u32[]{:S(2)}) collective-permute-start(bf16[512,384]{1,0:T(8,128)(2,1)} %select_convert_fusion), channel_id=1, source_target_pairs={{16,0},{17,1},{18,2},{19,3},{20,4},{21,5},{22,6},{23,7},{24,8},{25... | collective-permute-start | bytes 1179656 | tf_op jit(solution)/shard_map/ppermute | solution.py:16
  605.9 34.4 %copy-start.72 = (bf16[512,384]{0,1:T(8,128)(2,1)}, bf16[512,384]{0,1:T(8,128)(2,1)S(1)}, u32[]{:S(2)}) copy-start(bf16[512,384]{0,1:T(8,128)(2,1)S(1)} %get-tuple-element.2393) | copy-start | bytes 1179652
  605.9 34.4 %collective-permute-start.4 = (bf16[512,384]{0,1:T(8,128)(2,1)S(1)}, bf16[512,384]{0,1:T(8,128)(2,1)S(1)}, u32[]{:S(2)}, u32[]{:S(2)}) collective-permute-start(bf16[512,384]{0,1:T(8,128)(2,1)S(1)} %get-tuple-element.2393), channel_id=1, source_target_pairs={{0,16},{1,17},{2,18},{3,19},{4,20},{5,21},{6,22},{7,23},{8,24},{9,... | collective-permute-start | bytes 1179656 | tf_op jit(solution)/shard_map/ppermute | solution.py:16
  665.3 17.4 %copy-start.211 = (f32[512]{0:T(512)}, f32[512]{0:T(512)S(1)}, u32[]{:S(2)}) copy-start(f32[512]{0:T(512)S(1)} %broadcast_multiply_fusion.46) | copy-start | bytes 6148 | tf_op jit(solution)/shard_map/cond
  665.4 17.3 %copy-start.237 = (f32[512]{0:T(512)}, f32[512]{0:T(512)S(1)}, u32[]{:S(2)}) copy-start(f32[512]{0:T(512)S(1)} %add_rsqrt_fusion.22) | copy-start | bytes 6148 | tf_op jit(solution)/shard_map/cond
  800.0 10.9 %copy-start = (bf16[4,512,384]{2,1,0:T(8,128)(2,1)S(1)}, bf16[4,512,384]{2,1,0:T(8,128)(2,1)}, u32[]{:S(2)}) copy-start(bf16[4,512,384]{2,1,0:T(8,128)(2,1)} %param.44) | copy-start | bytes 4718596
  800.0 10.9 %copy-start.1 = (bf16[1,384,384]{2,1,0:T(8,128)(2,1)S(1)}, bf16[1,384,384]{2,1,0:T(8,128)(2,1)}, u32[]{:S(2)}) copy-start(bf16[1,384,384]{2,1,0:T(8,128)(2,1)} %param.52) | copy-start | bytes 884740
  800.0 10.9 %copy-start.39 = (f32[4,3,512]{2,0,1:T(4,128)S(1)}, f32[4,3,512]{2,0,1:T(4,128)}, u32[]{:S(2)}) copy-start(f32[4,3,512]{2,0,1:T(4,128)} %param.45) | copy-start | bytes 73732
  934.0 71.0 %copy-start.43 = (bf16[1,4,512,384]{3,2,1,0:T(8,128)(2,1)}, bf16[1,4,512,384]{3,2,1,0:T(8,128)(2,1)S(1)}, u32[]{:S(2)}) copy-start(bf16[1,4,512,384]{3,2,1,0:T(8,128)(2,1)S(1)} %bitcast_dynamic-update-slice_fusion.6) | copy-start | bytes 4718596
  (316 other events, 1537.6 us)
Sparse Core Ops, SparseCore 0:
  762.6 238.5 all-reduce.3
where the time goes:
time: 1030 us; the launch traced here: 1020 us
  matrix products  368 us (36%)
  local copies, waits for them, and re-layouts  170 us (17%)
  starting transfers between devices  140 us (14%)
  other arithmetic  123 us (12%)
  blocking collectives  119 us (12%)
  waiting for transfers between devices  70.5 us (7%)
  between operations  15.3 us (1%)
    ppermute x10, starting transfers between devices, shifted(): return lax.ppermute(block, axis, route)  140 us
    psum x1, blocking collectives, shards(): summed = list(lax.psum(tuple(totals), 'dp'))  76.4 us
    another operation x64, local copies, waits for them, and re-layouts  68.3 us
    dot_general x32, matrix products, matmul(): return jnp.dot(left_side, right_side, preferred_element_type=jnp.float32)  65.9 us
    psum x1, waiting for transfers between devices, shards(): summed = list(lax.psum(tuple(totals), 'dp'))  64.2 us
    sub x8, matrix products, attend(): raised = jnp.exp(scores - row_max)  51.4 us
    dot_general x20, matrix products, right_contract(): lax.dot_general(left_side, right_side, (((1,), (1,)), ((), ())), preferre...  51 us
    dot_general x4, matrix products, attend_back(): jnp.einsum('hqk,khd->qhd', grad_raw, keys_part, preferred_element_type=jn...  45.7 us
  transfers between devices with their start and end apart: 11, of which 6 were waited for; matrix products, arithmetic and copies ran while one was open for 16% of the time, Pallas kernels for 0%

commit v1 on v0

v1 whole, which is shorter than its diff:
```python
import math

import jax
import jax.numpy as jnp
from jax import lax
from jax.experimental import pallas as pl
from jax.experimental.pallas import tpu as pltpu
from jax.sharding import PartitionSpec as P

HEADS = 6
NEG_FILL = -1e30
NORM_EPS = 1e-05
GELU_A = math.sqrt(2.0 / math.pi)
GELU_B = GELU_A * 0.044715
BF = jnp.bfloat16
F32 = jnp.float32
VMEM_LIMIT = 56 * 2**20


def dot(a, b):
    return jnp.dot(a, b, preferred_element_type=F32)


def dot_rt(a, b):
    return lax.dot_general(a, b, (((1,), (1,)), ((), ())), preferred_element_type=F32)


def dot_lt(a, b):
    return lax.dot_general(a, b, (((0,), (0,)), ((), ())), preferred_element_type=F32)


def gelu_both(v):
    v2 = v * v
    h = 0.5 * jnp.tanh(v * (GELU_A + GELU_B * v2)) + 0.5
    slope = h + (h - h * h) * (v * (2.0 * GELU_A + 6.0 * GELU_B * v2))
    return v * h, slope


def gelu_only(v):
    return v * (0.5 * jnp.tanh(v * (GELU_A + GELU_B * (v * v))) + 0.5)


def norm_parts(x):
    scale = 1.0 / x.shape[-1]
    centred = x - jnp.sum(x, -1, keepdims=True) * scale
    var = jnp.sum(centred * centred, -1, keepdims=True) * scale
    inverse = lax.rsqrt(var + NORM_EPS)
    return centred * inverse, inverse


def norm_back(u, z, inverse, gain):
    scale = 1.0 / u.shape[-1]
    w = u * gain
    m1 = jnp.sum(w, -1, keepdims=True) * scale
    m2 = jnp.sum(w * z, -1, keepdims=True) * scale
    return inverse * (w - m1 - z * m2)


def place_pre(centre, place_weight, place_bias):
    pre = lax.dot_general(
        centre,
        place_weight,
        (((0,), (0,)), ((), ())),
        precision=lax.Precision.HIGHEST,
        preferred_element_type=F32,
    )
    return pre + place_bias


def column_of(row, width):
    rows = lax.broadcasted_iota(jnp.int32, (16, row.shape[1]), 0)
    top = jnp.where(rows == 0, jnp.broadcast_to(row, rows.shape), 0).astype(F32)
    return dot_lt(top.astype(BF), jnp.ones((16, width), BF))


def segments(lengths, micro_index, slots, places):
    total = jnp.int32(0)
    seg = jnp.zeros(places.shape, jnp.int32)
    for slot in range(slots):
        total = total + lengths[micro_index, slot]
        seg = seg + (places >= total).astype(jnp.int32)
    return seg


def lane_low(shape, half):
    return lax.broadcasted_iota(jnp.int32, shape, 1) < half


def attend_forward(decoding, rows_at_once, sel, lengths, *refs):
    (x_in, centres, visible, mask_token, ag, ash, wj, wo, bo, pw, pb, we) = refs[:12]
    (x_out, joint_out, e_out, inv_out, mixed_out, mid_out, bias) = refs[12:]
    step = pl.program_id(0)
    micro_index = sel[0] + step
    rows, width = x_in.shape[1], x_in.shape[2]
    slots = lengths.shape[1]
    head = width // HEADS
    pair = 2 * head

    pre = place_pre(centres[0], pw[...], pb[...])
    embed = dot(gelu_only(pre).astype(BF), we[...])
    seen = visible[pl.ds(micro_index, 1), :]
    source = x_in[0].astype(F32)
    if decoding:
        shown = column_of(seen, 128)[:, :1] > 0.5
        source = jnp.where(shown, source, mask_token[...])
    x = source + embed
    x_out[0] = x
    z, _ = norm_parts(x)
    low = (z * ag[...] + ash[...]).astype(BF)
    joint_out[0] = dot(low, wj[...]).astype(BF)

    places_k = lax.broadcasted_iota(jnp.int32, (1, rows), 1)
    seg_k = segments(lengths, micro_index, slots, places_k)
    seg_col = column_of(seg_k, 128)[:, :1].astype(jnp.int32)
    allowed = seg_col == seg_k
    if not decoding:
        places_q = lax.broadcasted_iota(jnp.int32, (rows, rows), 0)
        places_kk = lax.broadcasted_iota(jnp.int32, (rows, rows), 1)
        allowed = allowed & ((seen > 0) | (places_q == places_kk))
    bias[...] = jnp.where(allowed, 0.0, NEG_FILL)

    low_k = lane_low((rows, pair), head)
    low_q = lane_low((rows_at_once, pair), head)
    for p in range(HEADS // 2):
        qp = joint_out[0, :, p * pair : (p + 1) * pair] * BF(head**-0.5)
        kp = joint_out[0, :, width + p * pair : width + (p + 1) * pair]
        vp = joint_out[0, :, 2 * width + p * pair : 2 * width + (p + 1) * pair]
        v_low = jnp.where(low_k, vp, BF(1))
        v_high = jnp.where(low_k, BF(1), vp)
        for r0 in range(0, rows, rows_at_once):
            span = slice(r0, r0 + rows_at_once)
            q_rows = qp[span]
            out = []
            for side in range(2):
                q_one = jnp.where(low_q == (side == 0), q_rows, BF(0))
                s = dot_rt(q_one, kp) + bias[span, :]
                e = jnp.exp(s - jnp.max(s, -1, keepdims=True)).astype(BF)
                e_out[0, 2 * p + side, span, :] = e
                out.append(dot(e, v_high if side else v_low))
            inv = 1.0 / pltpu.roll(jnp.where(low_q, out[1], out[0]), head, 1)
            mixed = jnp.where(low_q, out[0], out[1]) * inv
            inv_out[0, span, p * pair : (p + 1) * pair] = inv
            mixed_out[0, span, p * pair : (p + 1) * pair] = mixed.astype(BF)
    mid_out[0] = x + (dot(mixed_out[0], wo[...]) + bo[...])


def attend_backward(decoding, rows_at_once, sel, lengths, *refs):
    (dmid_in, x_in, centres, visible, joint_in, e_in, inv_in, mixed_in) = refs[:8]
    (ag, ash, wj, wo, pw, pb, we) = refs[8:15]
    dx_out, send_back, joint_g, output_g, embed_g, small_g = refs[15:21]
    dl, mu, dj, ds = refs[21:25]
    step = pl.program_id(0)
    micro_index = sel[0] + step
    rows, width = x_in.shape[1], x_in.shape[2]
    head = width // HEADS
    pair = 2 * head
    hidden = pw.shape[1]

    @pl.when(step == 0)
    def _():
        joint_g[...] = jnp.zeros(joint_g.shape, F32)
        output_g[...] = jnp.zeros(output_g.shape, F32)
        embed_g[...] = jnp.zeros(embed_g.shape, F32)
        small_g[...] = jnp.zeros(small_g.shape, F32)

    dmid = dmid_in[0]
    dm = dmid.astype(BF)
    output_g[...] += dot_lt(mixed_in[0], dm)
    small_g[2:3, :] += jnp.sum(dm.astype(F32), 0, keepdims=True)
    dmix = dot_rt(dm, wo[...])
    low_dl = (dmix * inv_in[0]).astype(BF)
    dl[...] = low_dl
    mu[...] = (low_dl.astype(F32) * -mixed_in[0].astype(F32)).astype(BF)

    low_k = lane_low((rows, pair), head)
    ones = jnp.ones((rows, pair), BF)
    for p in range(HEADS // 2):
        cols = slice(p * pair, (p + 1) * pair)
        qp = joint_in[0, :, p * pair : (p + 1) * pair] * BF(head**-0.5)
        kp = joint_in[0, :, width + p * pair : width + (p + 1) * pair]
        vp = joint_in[0, :, 2 * width + p * pair : 2 * width + (p + 1) * pair]
        v_ext = jnp.concatenate([vp, ones], axis=1)
        dlp = dl[:, cols]
        mup = mu[:, cols]
        dq = dk = dv = None
        for side in range(2):
            mine = low_k == (side == 0)
            d_one = jnp.where(mine, dlp, BF(0))
            u_one = jnp.where(mine, mup, BF(0))
            ext = jnp.concatenate([d_one, u_one], axis=1)
            for r0 in range(0, rows, rows_at_once):
                span = slice(r0, r0 + rows_at_once)
                dp = dot_rt(ext[span], v_ext)
                ds[side, span, :] = (e_in[0, 2 * p + side, span, :].astype(F32) * dp).astype(BF)
            q_one = jnp.where(mine, qp, BF(0))
            k_one = jnp.where(mine, kp, BF(0))
            dv_one = dot_lt(e_in[0, 2 * p + side], d_one)
            dk_one = dot_lt(ds[side], q_one)
            dq_one = dot(ds[side], k_one)
            dv = dv_one if dv is None else dv + dv_one
            dk = dk_one if dk is None else dk + dk_one
            dq = dq_one if dq is None else dq + dq_one
        dj[:, p * pair : (p + 1) * pair] = (dq * head**-0.5).astype(BF)
        dj[:, width + p * pair : width + (p + 1) * pair] = dk.astype(BF)
        dj[:, 2 * width + p * pair : 2 * width + (p + 1) * pair] = dv.astype(BF)

    z, inverse = norm_parts(x_in[0])
    low = (z * ag[...] + ash[...]).astype(BF)
    joint_g[...] += dot_lt(low, dj[...])
    dn = dot_rt(dj[...], wj[...])
    small_g[0:1, :] += jnp.sum(dn * z, 0, keepdims=True)
    small_g[1:2, :] += jnp.sum(dn, 0, keepdims=True)
    dx = dmid + norm_back(dn, z, inverse, ag[...])
    dx_out[0] = dx
    if decoding:
        shown = column_of(visible[pl.ds(micro_index, 1), :], 128)[:, :1] > 0.5
        send_back[0] = jnp.where(shown, dx, 0.0).astype(BF)
        small_g[3:4, :] += jnp.sum(jnp.where(shown, 0.0, dx), 0, keepdims=True)

    pre = place_pre(centres[0], pw[...], pb[...])
    act, slope = gelu_both(pre)
    ge = dx.astype(BF)
    embed_g[...] += dot_lt(act.astype(BF), ge)
    dpre = slope * dot_rt(ge, we[...])
    place = jnp.dot(centres[0], dpre, precision=lax.Precision.HIGHEST, preferred_element_type=F32)
    small_g[4:7, 0:hidden] += place
    small_g[7:8, 0:hidden] += jnp.sum(dpre, 0, keepdims=True)


def feed_forward(mid_in, fg, fsh, w1, b1, w2, b2, out, act_out, slope_out, low, acc):
    step = pl.program_id(0)
    steps = pl.num_programs(0)

    @pl.when(step == 0)
    def _():
        z, _ = norm_parts(mid_in[...])
        low[...] = (z * fg[...] + fsh[...]).astype(BF)
        acc[...] = mid_in[...] + b2[...]

    hidden = dot(low[...], w1[...]) + b1[...]
    act, slope = gelu_both(hidden)
    act_low = act.astype(BF)
    act_out[...] = act_low
    slope_out[...] = slope.astype(BF)
    acc[...] += dot(act_low, w2[...])

    @pl.when(step == steps - 1)
    def _():
        out[...] = acc[...].astype(BF)


def feed_tail(g, dn_acc, mid_in, fg, dmid_out, small_g):
    z, inverse = norm_parts(mid_in[...])
    dn = dn_acc[...]
    dmid_out[...] = g + norm_back(dn, z, inverse, fg[...])
    small_g[0:1, :] = jnp.sum(dn * z, 0, keepdims=True)
    small_g[1:2, :] = jnp.sum(dn, 0, keepdims=True)
    small_g[2:3, :] = jnp.sum(g, 0, keepdims=True)


def feed_backward_chunk(low, act_low, slope, g, w1, w2, w1_g, w2_g, b1_g, dn_acc):
    dh = (slope * dot_rt(g, w2[...])).astype(BF)
    w2_g[...] = dot_lt(act_low, g)
    w1_g[...] = dot_lt(low, dh)
    b1_g[...] = jnp.sum(dh.astype(F32), 0, keepdims=True)
    dn_acc[...] += dot_rt(dh, w1[...])


def feed_both(mid_in, g_in, fg, fsh, w1, b1, w2, b2, out, dmid_out, w1_g, w2_g, b1_g, small_g, low, acc, dn_acc):
    step = pl.program_id(0)
    steps = pl.num_programs(0)

    @pl.when(step == 0)
    def _():
        z, _ = norm_parts(mid_in[...])
        low[...] = (z * fg[...] + fsh[...]).astype(BF)
        acc[...] = mid_in[...] + b2[...]
        dn_acc[...] = jnp.zeros(dn_acc.shape, F32)

    hidden = dot(low[...], w1[...]) + b1[...]
    act, slope = gelu_both(hidden)
    act_low = act.astype(BF)
    acc[...] += dot(act_low, w2[...])
    feed_backward_chunk(low[...], act_low, slope, g_in[...], w1, w2, w1_g, w2_g, b1_g, dn_acc)

    @pl.when(step == steps - 1)
    def _():
        out[...] = acc[...].astype(BF)
        feed_tail(g_in[...].astype(F32), dn_acc, mid_in, fg, dmid_out, small_g)


def feed_backward(mid_in, g_in, act_in, slope_in, fg, fsh, w1, w2, dmid_out, w1_g, w2_g, b1_g, small_g, low, dn_acc):
    step = pl.program_id(0)
    steps = pl.num_programs(0)

    @pl.when(step == 0)
    def _():
        z, _ = norm_parts(mid_in[...])
        low[...] = (z * fg[...] + fsh[...]).astype(BF)
        dn_acc[...] = jnp.zeros(dn_acc.shape, F32)

    feed_backward_chunk(low[...], act_in[...], slope_in[...].astype(F32), g_in[...], w1, w2, w1_g, w2_g, b1_g, dn_acc)

    @pl.when(step == steps - 1)
    def _():
        feed_tail(g_in[...].astype(F32), dn_acc, mid_in, fg, dmid_out, small_g)


def params():
    return pltpu.CompilerParams(vmem_limit_bytes=VMEM_LIMIT)


def whole(shape):
    return pl.BlockSpec(shape, lambda *_: (0,) * len(shape))


def sds(shape, kind):
    return jax.ShapeDtypeStruct(shape, kind)


def call_attend_forward(decoding, half, sel, lengths, x_in, centres, visible, mask_token, weights, rows_at_once=512):
    _, rows, width = x_in.shape
    ag, ash, wj, wo, bo, pw, pb, we = weights
    if decoding:
        x_spec = pl.BlockSpec((1, rows, width), lambda i, s, n: (i, 0, 0))
    else:
        x_spec = pl.BlockSpec((1, rows, width), lambda i, s, n: (s[0] + i, 0, 0))
    block = lambda *shape: pl.BlockSpec((1,) + shape, lambda i, s, n: (i,) + (0,) * len(shape))
    flops = 2 * rows * half * (width * 4 * width + 2 * HEADS * rows * 128)
    return pl.pallas_call(
        lambda *refs: attend_forward(decoding, rows_at_once, *refs),
        grid_spec=pltpu.PrefetchScalarGridSpec(
            num_scalar_prefetch=2,
            grid=(half,),
            in_specs=[
                x_spec,
                pl.BlockSpec((1,) + centres.shape[1:], lambda i, s, n: (s[0] + i, 0, 0)),
                whole(visible.shape),
                whole(mask_token.shape),
            ]
            + [whole(w.shape) for w in weights],
            out_specs=[
                block(rows, width),
                block(rows, 3 * width),
                block(HEADS, rows, rows),
                block(rows, width),
                block(rows, width),
                block(rows, width),
            ],
            scratch_shapes=[pltpu.VMEM((rows, rows), F32)],
        ),
        out_shape=[
            sds((half, rows, width), F32),
            sds((half, rows, 3 * width), BF),
            sds((half, HEADS, rows, rows), BF),
            sds((half, rows, width), F32),
            sds((half, rows, width), BF),
            sds((half, rows, width), F32),
        ],
        compiler_params=params(),
        cost_estimate=pl.CostEstimate(flops=flops, bytes_accessed=20 * 2**20, transcendentals=0),
        name="attend_forward_dec" if decoding else "attend_forward_enc",
    )(sel, lengths, x_in, centres, visible, mask_token, *weights)


def call_attend_backward(decoding, half, sel, lengths, dmid, x, centres, visible, joint, e, inv, mixed, weights, rows_at_once=512):
    _, rows, width = x.shape
    hidden = weights[4].shape[1]
    block = lambda *shape: pl.BlockSpec((1,) + shape, lambda i, s, n: (i,) + (0,) * len(shape))
    back = (half, rows, width) if decoding else (1, 16, width)
    return pl.pallas_call(
        lambda *refs: attend_backward(decoding, rows_at_once, *refs),
        grid_spec=pltpu.PrefetchScalarGridSpec(
            num_scalar_prefetch=2,
            grid=(half,),
            in_specs=[
                block(rows, width),
                block(rows, width),
                pl.BlockSpec((1,) + centres.shape[1:], lambda i, s, n: (s[0] + i, 0, 0)),
                whole(visible.shape),
                block(rows, 3 * width),
                block(HEADS, rows, rows),
                block(rows, width),
                block(rows, width),
            ]
            + [whole(w.shape) for w in weights],
            out_specs=[
                block(rows, width),
                block(rows, width) if decoding else whole(back),
                whole((width, 3 * width)),
                whole((width, width)),
                whole((hidden, width)),
                whole((8, width)),
            ],
            scratch_shapes=[
                pltpu.VMEM((rows, width), BF),
                pltpu.VMEM((rows, width), BF),
                pltpu.VMEM((rows, 3 * width), BF),
                pltpu.VMEM((2, rows, rows), BF),
            ],
        ),
        out_shape=[
            sds((half, rows, width), F32),
            sds(back, BF),
            sds((width, 3 * width), F32),
            sds((width, width), F32),
            sds((hidden, width), F32),
            sds((8, width), F32),
        ],
        compiler_params=params(),
        name="attend_backward_dec" if decoding else "attend_backward_enc",
    )(sel, lengths, dmid, x, centres, visible, joint, e, inv, mixed, *weights)


def feed_specs(rows, width, ff, chunk):
    w1 = pl.BlockSpec((width, chunk), lambda i: (0, i))
    b1 = pl.BlockSpec((1, chunk), lambda i: (0, i))
    w2 = pl.BlockSpec((chunk, width), lambda i: (i, 0))
    wide = pl.BlockSpec((rows, chunk), lambda i: (0, i))
    return w1, b1, w2, wide


def call_feed_forward(mid, fg, fsh, w1, b1, w2, b2, chunk=768):
    rows, width = mid.shape
    ff = w1.shape[1]
    s1, sb, s2, wide = feed_specs(rows, width, ff, chunk)
    row = whole((1, width))
    return pl.pallas_call(
        feed_forward,
        grid=(ff // chunk,),
        in_specs=[whole((rows, width)), row, row, s1, sb, s2, row],
        out_specs=[whole((rows, width)), wide, wide],
        out_shape=[sds((rows, width), BF), sds((rows, ff), BF), sds((rows, ff), BF)],
        scratch_shapes=[pltpu.VMEM((rows, width), BF), pltpu.VMEM((rows, width), F32)],
        compiler_params=params(),
        name="feed_forward_enc",
    )(mid, fg, fsh, w1, b1, w2, b2)


def call_feed_both(mid, g, fg, fsh, w1, b1, w2, b2, chunk=768):
    rows, width = mid.shape
    ff = w1.shape[1]
    s1, sb, s2, wide = feed_specs(rows, width, ff, chunk)
    row = whole((1, width))
    full = whole((rows, width))
    return pl.pallas_call(
        feed_both,
        grid=(ff // chunk,),
        in_specs=[full, full, row, row, s1, sb, s2, row],
        out_specs=[full, full, s1, s2, sb, whole((8, width))],
        out_shape=[
            sds((rows, width), BF),
            sds((rows, width), F32),
            sds((width, ff), F32),
            sds((ff, width), F32),
            sds((1, ff), F32),
            sds((8, width), F32),
        ],
        scratch_shapes=[pltpu.VMEM((rows, width), BF), pltpu.VMEM((rows, width), F32), pltpu.VMEM((rows, width), F32)],
        compiler_params=params(),
        name="feed_both_dec",
    )(mid, g, fg, fsh, w1, b1, w2, b2)


def call_feed_backward(mid, g, act, slope, fg, fsh, w1, w2, chunk=768):
    rows, width = mid.shape
    ff = w1.shape[1]
    s1, sb, s2, wide = feed_specs(rows, width, ff, chunk)
    row = whole((1, width))
    full = whole((rows, width))
    return pl.pallas_call(
        feed_backward,
        grid=(ff // chunk,),
        in_specs=[full, full, wide, wide, row, row, s1, s2],
        out_specs=[full, s1, s2, sb, whole((8, width))],
        out_shape=[
            sds((rows, width), F32),
            sds((width, ff), F32),
            sds((ff, width), F32),
            sds((1, ff), F32),
            sds((8, width), F32),
        ],
        scratch_shapes=[pltpu.VMEM((rows, width), BF), pltpu.VMEM((rows, width), F32)],
        compiler_params=params(),
        name="feed_backward_enc",
    )(mid, g, act, slope, fg, fsh, w1, w2)


def shards(
    tokens,
    centres,
    visible,
    lengths,
    cotangent,
    attend_gain,
    attend_shift,
    joint_weight,
    output_weight,
    output_bias,
    feed_gain,
    feed_shift,
    expand_weight,
    expand_bias,
    reduce_weight,
    reduce_bias,
    place_weight,
    place_bias,
    embed_weight,
    mask_token,
):
    phase = lax.axis_index("pipe")
    encoding = phase == 0
    micro, rows, width = tokens.shape
    half = micro // 2
    swap = [(0, 1), (1, 0)]
    own = [
        attend_gain, attend_shift, joint_weight[0], output_weight[0], output_bias, feed_gain, feed_shift,
        expand_weight[0], expand_bias, reduce_weight[0], reduce_bias, place_weight[0], place_bias, embed_weight[0],
    ]
    other = [lax.ppermute(piece, "pipe", swap) for piece in own]
    enc = [jnp.where(encoding, mine, theirs) for mine, theirs in zip(own, other)]
    dec = [jnp.where(encoding, theirs, mine) for mine, theirs in zip(own, other)]
    sel = jnp.reshape(phase * half, (1,)).astype(jnp.int32)
    mask_row = mask_token[None, :]
    given = lax.dynamic_slice_in_dim(cotangent, phase * half, half, 0).reshape(half * rows, width)

    def forward_weights(w):
        return [w[0], w[1], w[2], w[3], w[4], w[11], w[12], w[13]]

    def backward_weights(w):
        return [w[0], w[1], w[2], w[3], w[11], w[12], w[13]]

    ex, ej, ee, ei, em, emid = call_attend_forward(
        False, half, sel, lengths, tokens, centres, visible, mask_row, forward_weights(enc)
    )
    emid2 = emid.reshape(half * rows, width)
    enc_out, act, slope = call_feed_forward(emid2, enc[5], enc[6], enc[7], enc[8], enc[9], enc[10])
    enc_out = enc_out.reshape(half, rows, width)
    dx_, dj, de, di, dm, dmid = call_attend_forward(
        True, half, sel, lengths, enc_out, centres, visible, mask_row, forward_weights(dec)
    )
    dec_out, dback, d_w1, d_w2, d_b1, d_small = call_feed_both(
        dmid.reshape(half * rows, width), given, dec[5], dec[6], dec[7], dec[8], dec[9], dec[10]
    )
    ddx, enc_back, d_joint, d_output, d_embed, d_small2 = call_attend_backward(
        True, half, sel, lengths, dback.reshape(half, rows, width), dx_, centres, visible, dj, de, di, dm,
        backward_weights(dec),
    )
    eback, e_w1, e_w2, e_b1, e_small = call_feed_backward(
        emid2, enc_back.reshape(half * rows, width), act, slope, enc[5], enc[6], enc[7], enc[9]
    )
    edx, _, e_joint, e_output, e_embed, e_small2 = call_attend_backward(
        False, half, sel, lengths, eback.reshape(half, rows, width), ex, centres, visible, ej, ee, ei, em,
        backward_weights(enc),
    )

    def grads(joint, output, embed, w1, b1, w2, small, small2):
        hidden = place_weight.shape[2]
        return [
            small2[0], small2[1], joint, output, small2[2], small[0], small[1], w1, b1[0], w2, small[2],
            small2[4:7, :hidden], small2[7, :hidden], embed,
        ]

    g_enc = grads(e_joint, e_output, e_embed, e_w1, e_b1, e_w2, e_small, e_small2)
    g_dec = grads(d_joint, d_output, d_embed, d_w1, d_b1, d_w2, d_small, d_small2)
    mine = [jnp.where(encoding, a, b) for a, b in zip(g_enc, g_dec)]
    sent = [jnp.where(encoding, b, a) for a, b in zip(g_enc, g_dec)]
    came = [lax.ppermute(piece, "pipe", swap) for piece in sent]
    summed = list(lax.psum(tuple(a + b for a, b in zip(mine, came)), "dp"))
    mask_grad = lax.psum(d_small2[3], ("pipe", "dp"))

    def joined(enc_part, dec_part):
        got = lax.ppermute(jnp.where(encoding, dec_part, enc_part), "pipe", swap)
        first = jnp.where(encoding, enc_part, got)
        second = jnp.where(encoding, got, dec_part)
        return jnp.concatenate([first, second], 0)[None]

    phase_out = joined(enc_out, dec_out.reshape(half, rows, width))
    phase_in_grad = joined(edx, ddx)
    return tuple([phase_out, phase_in_grad] + [piece[None] for piece in summed] + [mask_grad])


def solution(mesh):
    in_specs = (
        P(None, "dp", None),
        P(None, None, "dp"),
        P(None, "dp"),
        P(None, "dp"),
        P(None, "dp", None),
        P("pipe", None),
        P("pipe", None),
        P("pipe", None, None),
        P("pipe", None, None),
        P("pipe", None),
        P("pipe", None),
        P("pipe", None),
        P("pipe", None, None),
        P("pipe", None),
        P("pipe", None, None),
        P("pipe", None),
        P("pipe", None, None),
        P("pipe", None),
        P("pipe", None, None),
        P(),
    )
    out_specs = (
        P("pipe", None, "dp", None),
        P("pipe", None, "dp", None),
        P("pipe", None),
        P("pipe", None),
        P("pipe", None, None),
        P("pipe", None, None),
        P("pipe", None),
        P("pipe", None),
        P("pipe", None),
        P("pipe", None, None),
        P("pipe", None),
        P("pipe", None, None),
        P("pipe", None),
        P("pipe", None, None),
        P("pipe", None),
        P("pipe", None, None),
        P(),
    )
    return jax.shard_map(shards, mesh=mesh, in_specs=in_specs, out_specs=out_specs, check_vma=False)
```

time: 1030 us -> 428 us (0.42)
  matrix products: 368 us -> 0 us
  local copies, waits for them, and re-layouts: 170 us -> 16.6 us
  starting transfers between devices: 140 us -> 12.6 us
  Pallas kernels: 0 us -> 110 us
  other arithmetic: 123 us -> 35 us
  waiting for transfers between devices: 70.5 us -> 109 us
    dot_general x96 -> x0, matrix products: 316 us -> none  [the longest x32 65.9 us: matmul(): return jnp.dot(left_side, right_side, preferred_element_type=jnp.float32)]
    ppermute x10 -> x30, starting transfers between devices: 140 us -> 12.6 us  [the longest x14 8.24 us: shards(): came = [lax.ppermute(piece, 'pipe', swap) for piece in sent]]
    pallas_call x0 -> x7, Pallas kernels: none -> 110 us  [the longest x2 40.2 us: call_attend_backward(): pl.pallas_call(lambda *refs: attend_backward(decoding, rows_at_once, *ref...]
    another operation x64 -> x0, local copies, waits for them, and re-layouts: 68.3 us -> none
    sub x8 -> x0, matrix products: 51.4 us -> none  [attend(): raised = jnp.exp(scores - row_max)]
    reduce_sum x46 -> x0, other arithmetic: 43.2 us -> none  [the longest x6 9.63 us: shards(): jnp.sum(jnp.where(visible_block[:, None] > 0, 0.0, grad_inputs), 0)]
    psum x1, waiting for transfers between devices: 64.2 us -> 102 us  [shards(): summed = list(lax.psum(tuple((a + b for a, b in zip(mine, came))), 'dp'))]
    cond x557 -> x0, local copies, waits for them, and re-layouts: 26.9 us -> none
  transfers between devices with their start and end apart: 11 -> 31, of which waited for: 6 -> 6; matrix products, arithmetic and copies ran while one was open for 16% -> 9% of each run, Pallas kernels for 0% -> 3%
where the time goes in v1:
time: 428 us; the launch traced here: 420 us
  blocking collectives  122 us (29%)
  Pallas kernels  110 us (26%)
  waiting for transfers between devices  109 us (25%)
  other arithmetic  35 us (8%)
  local copies, waits for them, and re-layouts  16.6 us (4%)
  between operations  14.8 us (3%)
  starting transfers between devices  12.6 us (3%)
    psum x1, waiting for transfers between devices, shards(): summed = list(lax.psum(tuple((a + b for a, b in zip(mine, came))), 'dp'))  102 us
    psum x1, blocking collectives, shards(): summed = list(lax.psum(tuple((a + b for a, b in zip(mine, came))), 'dp'))  76.5 us
    psum x1, blocking collectives, shards(): mask_grad = lax.psum(d_small2[3], ('pipe', 'dp'))  45.5 us
    pallas_call x2, Pallas kernels, call_attend_backward(): pl.pallas_call(lambda *refs: attend_backward(decoding, rows_at_once, *ref...  40.2 us
    pallas_call x2, Pallas kernels, call_attend_forward(): pl.pallas_call(lambda *refs: attend_forward(decoding, rows_at_once, *refs...  29 us
    select_n x14, other arithmetic, shards(): jnp.where(encoding, theirs, mine)  17.5 us
    pallas_call x1, Pallas kernels, call_feed_both(): pl.pallas_call(feed_both, grid=(ff // chunk,), in_specs=[full, full, row,...  17 us
    unnamed x66, local copies, waits for them, and re-layouts  14.3 us
  transfers between devices with their start and end apart: 31, of which 6 were waited for; matrix products, arithmetic and copies ran while one was open for 9% of the time, Pallas kernels for 3%

profile of v1, /device:TPU:0, one launch (start us, length us, event | category | flops | bytes accessed | tf_op | source)
XLA Modules:
  0.0 419.8 jit_solution(2178085735390859657)
XLA Ops:
  11.7 1.4 copy.37.refs_3_.refs_4_
  14.8 1.3 broadcast_select_fusion.53
  20.9 1.3 broadcast_select_fusion.39
  25.5 1.3 broadcast_select_fusion.23
  28.4 1.4 broadcast_select_fusion.7
  29.7 14.6 %attend_forward_enc.1 = (f32[2,512,384]{2,1,0:T(8,128)}, bf16[2,512,1152]{2,1,0:T(8,128)(2,1)}, bf16[2,6,512,512]{3,2,1,0:T(8,128)(2,1)}, f32[2,512,384]{2,1,0:T...) custom-call(s32[1]{0:T(128)} %bitcast.refs_0_, s32[4,8]{1,0:T(4,128)} %refs_1_.7, ...), custom_call_target="tpu_custom_call" | custom-call | flops 2818572288 | bytes 20971520 | tf_op jit(solution)/shard_map/attend_forward_enc/pallas_call | solution.py:330
  44.4 1.6 broadcast_select_fusion.1
  46.0 1.6 broadcast_select_fusion.4
  47.6 10.1 %feed_forward_enc.1 = (bf16[1024,384]{1,0:T(8,128)(2,1)}, bf16[1024,1536]{1,0:T(8,128)(2,1)}, bf16[1024,1536]{1,0:T(8,128)(2,1)}) custom-call(f32[1024,384]{1,0:T(8,128)} %bitcast.57, f32[1,384]{1,0:T(1,128)} %get-tuple-element.160.fg, f32[1,384]{1,0:T(1,128)} %get-tuple-element.158.fsh, bf16[384,1536]{1,0:T(8,128)(2,1)} %get-tuple-element.140.w1, ...), custom_call_target="tpu_custom_call" | custom-call | tf_op jit(solution)/shard_map/feed_forward_enc/pallas_call | solution.py:428
  57.7 14.4 %attend_forward_dec.1 = (f32[2,512,384]{2,1,0:T(8,128)}, bf16[2,512,1152]{2,1,0:T(8,128)(2,1)}, bf16[2,6,512,512]{3,2,1,0:T(8,128)(2,1)}, f32[2,512,384]{2,1,0:T...) custom-call(s32[1]{0:T(128)} %bitcast.refs_0_, s32[4,8]{1,0:T(4,128)} %refs_1_.7, ...), custom_call_target="tpu_custom_call" | custom-call | flops 2818572288 | bytes 20971520 | tf_op jit(solution)/shard_map/attend_forward_dec/pallas_call | solution.py:330
  72.1 17.0 %feed_both_dec.1 = (bf16[1024,384]{1,0:T(8,128)(2,1)}, f32[1024,384]{1,0:T(8,128)}, f32[384,1536]{1,0:T(8,128)}, f32[1536,384]{1,0:T(8,128)}, f32[1,1536]{1,0:T(1,128)}, /*index=5*/f32[8,384]{1,0:T(8,128)}) custom-call(f32[1024,384]{1,0:T(8,128)} %bitcast.67, bf16[1024,384]{1,0:T(8,128)(2,1)} %bitcast.59, f32[1,384]{1,0:T(1,128)} %get-tuple-element.159.fg, ...), custom_call_target="tpu_custom_call" | custom-call | tf_op jit(solution)/shard_map/feed_both_dec/pallas_call | solution.py:446
  89.1 20.0 %attend_backward_dec.1 = (f32[2,512,384]{2,1,0:T(8,128)}, bf16[2,512,384]{2,1,0:T(8,128)(2,1)}, f32[384,1152]{1,0:T(8,128)}, f32[384,384]{1,0:T(8,128)}, f32[128,384]{1,0:T(8,128)}, /*index=5*/f32[8,384]{1,0:T(8,128)}) custom-call(s32[1]{0:T(128)} %bitcast.refs_0_, s32[4,8]{1,0:T(4,128)} %refs_1_.7, f32[2,512,384]{2,1,0:T(8,128)} %bitcast.66, ...), custom_call_target="tpu_custom_call" | custom-call | tf_op jit(solution)/shard_map/attend_backward_dec/pallas_call | solution.py:371
  109.2 13.6 %feed_backward_enc.1 = (f32[1024,384]{1,0:T(8,128)}, f32[384,1536]{1,0:T(8,128)}, f32[1536,384]{1,0:T(8,128)}, f32[1,1536]{1,0:T(1,128)}, f32[8,384]{1,0:T(8,128)}) custom-call(f32[1024,384]{1,0:T(8,128)} %bitcast.58, bf16[1024,384]{1,0:T(8,128)(2,1)} %bitcast.71, bf16[1024,1536]{1,0:T(8,128)(2,1)} %get-tuple-element.65.act_in, ...), custom_call_target="tpu_custom_call" | custom-call | tf_op jit(solution)/shard_map/feed_backward_enc/pallas_call | solution.py:471
  122.8 20.1 %attend_backward_enc.1 = (f32[2,512,384]{2,1,0:T(8,128)}, bf16[1,16,384]{2,1,0:T(8,128)(2,1)}, f32[384,1152]{1,0:T(8,128)}, f32[384,384]{1,0:T(8,128)}, f32[128,384]{1,0:T(8,128)}, /*index=5*/f32[8,384]{1,0:T(8,128)}) custom-call(s32[1]{0:T(128)} %bitcast.refs_0_, s32[4,8]{1,0:T(4,128)} %refs_1_.7, f32[2,512,384]{2,1,0:T(8,128)} %bitcast.65, ...), custom_call_target="tpu_custom_call" | custom-call | tf_op jit(solution)/shard_map/attend_backward_enc/pallas_call | solution.py:371
  143.0 1.5 collective-permute-start.19
  144.8 2.0 collective-permute-start.18
  151.3 5.8 %collective-permute-done.29 = f32[128,384]{1,0:T(8,128)S(1)} collective-permute-done((f32[128,384]{1,0:T(8,128)S(1)}, f32[128,384]{1,0:T(8,128)S(1)}, u32[]{:S(2)}, u32[]{:S(2)}) %collective-permute-start.29) | collective-permute-done | bytes 196640 | tf_op jit(solution)/shard_map/ppermute | solution.py:568
  158.7 1.5 add_bitcast_fusion.2
  160.2 1.7 add_bitcast_fusion
  162.0 2.1 add_bitcast_fusion.1
  164.1 1.4 copy-done.8
  166.0 1.3 broadcast_select_fusion.11
  170.8 45.5 %psum.119 = f32[384]{0:T(512)} all-reduce(f32[384]{0:T(512)S(1)} %get-tuple-element.120), channel_id=1, replica_groups=mesh['pipe'=2,'dp'=16] {'pipe','dp'}, use_global_device_ids=true, to_apply=%region_14.15 | all-reduce | flops 384 | bytes 3072 | tf_op jit(solution)/shard_map/psum | solution.py:570
  219.2 76.5 %all-reduce = (f32[1,384]{1,0:T(1,128)}, f32[1,384]{1,0:T(1,128)}, f32[1,384]{1,0:T(1,128)}, f32[1,384]{1,0:T(1,128)}, f32[1,384]{1,0:T(1,128)}, /*index=5*/f32[...) all-reduce(f32[1,384]{1,0:T(1,128)S(1)} %broadcast_in_dim.54, ...), channel_id=1, replica_groups=mesh['pipe'=2,'dp'=16] {'dp'}, use_global_device_ids=true, to_apply=%region_0.1 | all-reduce | flops 4352 | bytes 34816 | tf_op jit(solution)/shard_map/psum | solution.py:569
  296.2 1.5 broadcast_select_fusion.13
  297.8 1.3 maximum_bitcast_fusion.1
  299.1 1.7 broadcast_select_fusion.10
  300.8 1.9 maximum_bitcast_fusion
  302.6 101.5 %all-reduce.4.cloned.1.call-done = (f32[1,384,1152]{2,1,0:T(8,128)}, f32[1,384,384]{2,1,0:T(8,128)}, f32[1,384,1536]{2,1,0:T(8,128)}, f32[1,1536,384]{2,1,0:T(8,128)}, f32[1,128,384]{2,1,0:T(8,128)}) async-done(((f32[1,384,1152]{2,1,0:T(8,128)}, f32[1,384,384]{2,1,0:T(8,128)}, f32[1,384,1536]{2,1,0:T(8,128)}, f32[1,1536,384]{2,1,0:T(8,128)}, f32[1,128,384]{2,1,0:T(8,128)}), (f32[1,384,1152]{2,1,0:T(8,128)}, ...) | async-done | bytes 7274512 | tf_op jit(solution)/shard_map/psum | solution.py:569
  404.2 2.9 copy.54
  407.9 1.4 copy.56
  410.4 1.4 copy.57
  (159 shorter events, 32.3 us)
Async XLA Ops:
  7.2 21.1 %copy-start.18 = (bf16[1,384,1152]{2,1,0:T(8,128)(2,1)S(1)}, bf16[1,384,1152]{2,1,0:T(8,128)(2,1)}, u32[]{:S(2)}) copy-start(bf16[1,384,1152]{2,1,0:T(8,128)(2,1)} %param.27) | copy-start | bytes 2654212
  7.2 396.9 %all-reduce.4.cloned.1.call-start = ((), (), s32[]{:S(2)}) async-start(), calls=%async_computation | async-start | bytes 14548992 | tf_op jit(solution)/shard_map/psum | solution.py:569
  7.3 5.8 %collective-permute-start.6 = (f32[1,128]{1,0:T(1,128)}, f32[1,128]{1,0:T(1,128)S(1)}, u32[]{:S(2)}, u32[]{:S(2)}) collective-permute-start(f32[1,128]{1,0:T(1,128)} %param.37), channel_id=1, source_target_pairs={{0,16},{16,0},{1,17},{17,1},{2,18},{18,2},{3,19},{19,3},{4,20},{20... | collective-permute-start | bytes 1544 | tf_op jit(solution)/shard_map/ppermute | solution.py:520
  7.8 8.3 %collective-permute-start = (f32[1,384]{1,0:T(1,128)}, f32[1,384]{1,0:T(1,128)S(1)}, u32[]{:S(2)}, u32[]{:S(2)}) collective-permute-start(f32[1,384]{1,0:T(1,128)} %param.25), channel_id=1, source_target_pairs={{0,16},{16,0},{1,17},{17,1},{2,18},{18,2},{3,19},{19,3},{4,20},{20... | collective-permute-start | bytes 4616 | tf_op jit(solution)/shard_map/ppermute | solution.py:520
  7.9 9.7 %collective-permute-start.1 = (f32[1,384]{1,0:T(1,128)}, f32[1,384]{1,0:T(1,128)S(1)}, u32[]{:S(2)}, u32[]{:S(2)}) collective-permute-start(f32[1,384]{1,0:T(1,128)} %param.26), channel_id=1, source_target_pairs={{0,16},{16,0},{1,17},{17,1},{2,18},{18,2},{3,19},{19,3},{4,20},{20... | collective-permute-start | bytes 4616 | tf_op jit(solution)/shard_map/ppermute | solution.py:520
  8.3 10.8 %collective-permute-start.4 = (f32[1,384]{1,0:T(1,128)}, f32[1,384]{1,0:T(1,128)S(1)}, u32[]{:S(2)}, u32[]{:S(2)}) collective-permute-start(f32[1,384]{1,0:T(1,128)} %param.29), channel_id=1, source_target_pairs={{0,16},{16,0},{1,17},{17,1},{2,18},{18,2},{3,19},{19,3},{4,20},{20... | collective-permute-start | bytes 4616 | tf_op jit(solution)/shard_map/ppermute | solution.py:520
  8.4 12.2 %collective-permute-start.8 = (f32[1,384]{1,0:T(1,128)}, f32[1,384]{1,0:T(1,128)S(1)}, u32[]{:S(2)}, u32[]{:S(2)}) collective-permute-start(f32[1,384]{1,0:T(1,128)} %param.30), channel_id=1, source_target_pairs={{0,16},{16,0},{1,17},{17,1},{2,18},{18,2},{3,19},{19,3},{4,20},{20... | collective-permute-start | bytes 4616 | tf_op jit(solution)/shard_map/ppermute | solution.py:520
  13.1 1.4 collective-permute-start.5
  14.5 7.6 %collective-permute-start.9 = (f32[1,384]{1,0:T(1,128)}, f32[1,384]{1,0:T(1,128)S(1)}, u32[]{:S(2)}, u32[]{:S(2)}) collective-permute-start(f32[1,384]{1,0:T(1,128)} %param.31), channel_id=1, source_target_pairs={{0,16},{16,0},{1,17},{17,1},{2,18},{18,2},{3,19},{19,3},{4,20},{20... | collective-permute-start | bytes 4616 | tf_op jit(solution)/shard_map/ppermute | solution.py:520
  16.1 7.6 %collective-permute-start.13 = (f32[1,384]{1,0:T(1,128)}, f32[1,384]{1,0:T(1,128)S(1)}, u32[]{:S(2)}, u32[]{:S(2)}) collective-permute-start(f32[1,384]{1,0:T(1,128)} %param.35), channel_id=1, source_target_pairs={{0,16},{16,0},{1,17},{17,1},{2,18},{18,2},{3,19},{19,3},{4,20},{20... | collective-permute-start | bytes 4616 | tf_op jit(solution)/shard_map/ppermute | solution.py:520
  17.6 7.6 %collective-permute-start.11 = (f32[1,1536]{1,0:T(1,128)}, f32[1,1536]{1,0:T(1,128)S(1)}, u32[]{:S(2)}, u32[]{:S(2)}) collective-permute-start(f32[1,1536]{1,0:T(1,128)} %param.33), channel_id=1, source_target_pairs={{0,16},{16,0},{1,17},{17,1},{2,18},{18,2},{3,19},{19,3},{4,20},{20... | collective-permute-start | bytes 18440 | tf_op jit(solution)/shard_map/ppermute | solution.py:520
  19.1 7.6 %collective-permute-start.7 = (bf16[128,384]{1,0:T(8,128)(2,1)}, bf16[128,384]{1,0:T(8,128)(2,1)S(1)}, u32[]{:S(2)}, u32[]{:S(2)}) collective-permute-start(bf16[128,384]{1,0:T(8,128)(2,1)} %bitcast.73), channel_id=1, source_target_pairs={{0,16},{16,0},{1,17},{17,1},{2,18},{18,2},{3,19},{19,3},{4,20},{20... | collective-permute-start | bytes 294920 | tf_op jit(solution)/shard_map/ppermute | solution.py:520
  20.6 6.9 %collective-permute-start.3 = (bf16[384,384]{1,0:T(8,128)(2,1)}, bf16[384,384]{1,0:T(8,128)(2,1)S(1)}, u32[]{:S(2)}, u32[]{:S(2)}) collective-permute-start(bf16[384,384]{1,0:T(8,128)(2,1)} %bitcast.72), channel_id=1, source_target_pairs={{0,16},{16,0},{1,17},{17,1},{2,18},{18,2},{3,19},{19,3},{4,20},{20... | collective-permute-start | bytes 884744 | tf_op jit(solution)/shard_map/ppermute | solution.py:520
  22.2 6.2 %collective-permute-start.2 = (bf16[384,1152]{1,0:T(8,128)(2,1)}, bf16[384,1152]{1,0:T(8,128)(2,1)S(1)}, u32[]{:S(2)}, u32[]{:S(2)}) collective-permute-start(bf16[384,1152]{1,0:T(8,128)(2,1)} %bitcast.70), channel_id=1, source_target_pairs={{0,16},{16,0},{1,17},{17,1},{2,18},{18,2},{3,19},{19,3},{4,20},{20... | collective-permute-start | bytes 2654216 | tf_op jit(solution)/shard_map/ppermute | solution.py:520
  23.7 20.7 %collective-permute-start.12 = (bf16[1536,384]{1,0:T(8,128)(2,1)}, bf16[1536,384]{1,0:T(8,128)(2,1)S(1)}, u32[]{:S(2)}, u32[]{:S(2)}) collective-permute-start(bf16[1536,384]{1,0:T(8,128)(2,1)} %bitcast.68), channel_id=1, source_target_pairs={{0,16},{16,0},{1,17},{17,1},{2,18},{18,2},{3,19},{19,3},{4,20},{20... | collective-permute-start | bytes 3538952 | tf_op jit(solution)/shard_map/ppermute | solution.py:520
  25.2 20.8 %collective-permute-start.10 = (bf16[384,1536]{1,0:T(8,128)(2,1)}, bf16[384,1536]{1,0:T(8,128)(2,1)S(1)}, u32[]{:S(2)}, u32[]{:S(2)}) collective-permute-start(bf16[384,1536]{1,0:T(8,128)(2,1)} %bitcast.69), channel_id=1, source_target_pairs={{0,16},{16,0},{1,17},{17,1},{2,18},{18,2},{3,19},{19,3},{4,20},{20... | collective-permute-start | bytes 3538952 | tf_op jit(solution)/shard_map/ppermute | solution.py:520
  143.0 14.8 %collective-permute-start.19 = (f32[384,384]{1,0:T(8,128)S(1)}, f32[384,384]{1,0:T(8,128)S(1)}, u32[]{:S(2)}, u32[]{:S(2)}) collective-permute-start(f32[384,384]{1,0:T(8,128)S(1)} %broadcast_select_fusion.15), channel_id=1, source_target_pairs={{0,16},{16,0},{1,17},{17,1},{2,18},{18,2},{3,19},{19,3},{4,20},{20... | collective-permute-start | bytes 1769480 | tf_op jit(solution)/shard_map/ppermute | solution.py:568
  144.8 14.0 %collective-permute-start.18 = (f32[384,1152]{1,0:T(8,128)S(1)}, f32[384,1152]{1,0:T(8,128)S(1)}, u32[]{:S(2)}, u32[]{:S(2)}) collective-permute-start(f32[384,1152]{1,0:T(8,128)S(1)} %broadcast_select_fusion.6), channel_id=1, source_target_pairs={{0,16},{16,0},{1,17},{17,1},{2,18},{18,2},{3,19},{19,3},{4,20},{20... | collective-permute-start | bytes 5308424 | tf_op jit(solution)/shard_map/ppermute | solution.py:568
  147.2 13.0 %collective-permute-start.25 = (f32[1536,384]{1,0:T(8,128)S(1)}, f32[1536,384]{1,0:T(8,128)S(1)}, u32[]{:S(2)}, u32[]{:S(2)}) collective-permute-start(f32[1536,384]{1,0:T(8,128)S(1)} %broadcast_select_fusion), channel_id=1, source_target_pairs={{0,16},{16,0},{1,17},{17,1},{2,18},{18,2},{3,19},{19,3},{4,20},{20... | collective-permute-start | bytes 7077896 | tf_op jit(solution)/shard_map/ppermute | solution.py:568
  149.7 12.2 %collective-permute-start.23 = (f32[384,1536]{1,0:T(8,128)S(1)}, f32[384,1536]{1,0:T(8,128)S(1)}, u32[]{:S(2)}, u32[]{:S(2)}) collective-permute-start(f32[384,1536]{1,0:T(8,128)S(1)} %broadcast_select_fusion.3), channel_id=1, source_target_pairs={{0,16},{16,0},{1,17},{17,1},{2,18},{18,2},{3,19},{19,3},{4,20},{20... | collective-permute-start | bytes 7077896 | tf_op jit(solution)/shard_map/ppermute | solution.py:568
  150.7 6.5 %collective-permute-start.29 = (f32[128,384]{1,0:T(8,128)S(1)}, f32[128,384]{1,0:T(8,128)S(1)}, u32[]{:S(2)}, u32[]{:S(2)}) collective-permute-start(f32[128,384]{1,0:T(8,128)S(1)} %broadcast_select_fusion.18), channel_id=1, source_target_pairs={{0,16},{16,0},{1,17},{17,1},{2,18},{18,2},{3,19},{19,3},{4,20},{20... | collective-permute-start | bytes 589832 | tf_op jit(solution)/shard_map/ppermute | solution.py:568
  167.3 131.8 %collective-permute-start.15 = (f32[2,512,384]{2,1,0:T(8,128)}, f32[2,512,384]{2,1,0:T(8,128)}, u32[]{:S(2)}, u32[]{:S(2)}) collective-permute-start(f32[2,512,384]{2,1,0:T(8,128)} %broadcast_select_fusion.11), channel_id=1, source_target_pairs={{0,16},{16,0},{1,17},{17,1},{2,18},{18,2},{3,19},{19,3},{4,20},{20... | collective-permute-start | bytes 4718600 | tf_op jit(solution)/shard_map/ppermute | solution.py:573
  167.7 48.7 %collective-permute-start.28 = (f32[128]{0:T(128)S(1)}, f32[128]{0:T(128)S(1)}, u32[]{:S(2)}, u32[]{:S(2)}) collective-permute-start(f32[128]{0:T(128)S(1)} %fusion.17), channel_id=1, source_target_pairs={{0,16},{16,0},{1,17},{17,1},{2,18},{18,2},{3,19},{19,3},{4,20},{20... | collective-permute-start | bytes 1544 | tf_op jit(solution)/shard_map/ppermute | solution.py:568
  167.9 48.5 %collective-permute-start.27 = (f32[3,128]{1,0:T(4,128)S(1)}, f32[3,128]{1,0:T(4,128)S(1)}, u32[]{:S(2)}, u32[]{:S(2)}) collective-permute-start(f32[3,128]{1,0:T(4,128)S(1)} %slice_select_fusion), channel_id=1, source_target_pairs={{0,16},{16,0},{1,17},{17,1},{2,18},{18,2},{3,19},{19,3},{4,20},{20... | collective-permute-start | bytes 4616 | tf_op jit(solution)/shard_map/ppermute | solution.py:568
  169.2 127.0 %collective-permute-start.14 = (bf16[2,512,384]{2,1,0:T(8,128)(2,1)}, bf16[2,512,384]{2,1,0:T(8,128)(2,1)}, u32[]{:S(2)}, u32[]{:S(2)}) collective-permute-start(bf16[2,512,384]{2,1,0:T(8,128)(2,1)} %broadcast_select_fusion.14), channel_id=1, source_target_pairs={{0,16},{16,0},{1,17},{17,1},{2,18},{18,2},{3,19},{19,3},{4,20},{20... | collective-permute-start | bytes 2359304 | tf_op jit(solution)/shard_map/ppermute | solution.py:573
  169.4 47.4 %collective-permute-start.20 = (f32[384]{0:T(512)S(1)}, f32[384]{0:T(512)S(1)}, u32[]{:S(2)}, u32[]{:S(2)}) collective-permute-start(f32[384]{0:T(512)S(1)} %get-tuple-element.114), channel_id=1, source_target_pairs={{0,16},{16,0},{1,17},{17,1},{2,18},{18,2},{3,19},{19,3},{4,20},{20... | collective-permute-start | bytes 4616 | tf_op jit(solution)/shard_map/ppermute | solution.py:568
  216.3 1.2 collective-permute-start.16
  216.4 1.3 collective-permute-start.17
  216.8 1.2 collective-permute-start.26
  217.5 1.2 collective-permute-start.21
  217.7 1.2 collective-permute-start.22
  218.0 1.2 collective-permute-start.24
  (28 other events, 140.4 us)
Sparse Core Ops, SparseCore 0:
  164.2 239.8 all-reduce.3
